TPU v7x, 32 devices: a whole 2x2x4 slice. The times are simulated.
32 devices in a mesh: grp: 4 (over z), pen: 8 (over y, x, core).
Axes of the slice: x: 2, y: 2, z: 4, core: 2. Of those that a mesh axis runs over, the one named last changes fastest.
Arguments:
- psi: float32 [2, 512, 128, 512], P(None, 'pen', 'grp'), may hold values from -6 to 6
- potential: float32 [512, 128, 512], P('pen', 'grp'), may hold values from -20 to 20
- absorber_region: int32 [512, 128], P('pen', 'grp'), may hold values from 0 to 3
- absorber_strength: float32 [4], replicated, may hold values from 0.5 to 8
- route_owner: int32 [4, 8, 2048, 2], P('grp', 'pen'), may hold values from 0 to 7, all different within a row; in each aligned block of 2048 rows (0 to 2047, 2048 to 4095, ..., all dimensions but the last counted through in order) at most 1024 rows name the same one
- route_row: int32 [4, 8, 2048, 2], P('grp', 'pen'), may hold values from 0 to 63
- route_weight: float32 [4, 8, 2048, 2], P('grp', 'pen'), may hold values from 0.25 to 1
Outputs:
- psi_final: float32 [2, 512, 128, 512], P(None, 'pen', 'grp')
- product_flux: float32 [4, 8, 64, 256], P('grp', 'pen')
Inputs may be any that keep to these rules, and one draw needn't show every extreme that they name: `route_owner`: in each device's 2048 rows (aligned blocks of 2048 rows) no owner is named by more than 1024 rows, a bound that some block reaches; the two owners of a row differ.
All inputs are finite; a program needn't handle non-finite values.
Results may differ from a plain program's by a relative error of at most 0.029.
Values may be sent and summed in bfloat16 or wider, within the bound.
A program may use at most 128 MiB of HBM per device.

v0:
```python
import math

import jax
import jax.numpy as jnp
from jax import lax
from jax.sharding import PartitionSpec as P

NS = 512
NL = 512
NANG = 128
RABS = 128
STEPS = 2
NREGION = 4
PSROWS = 64


time_step = 0.05
grid_spacing = 0.1
reduced_mass = 0.999456
energy_cap = 500.0


def sine_table(count):
    counter = jnp.arange(count, dtype=jnp.int32) + 1
    product = counter[:, None] * counter[None, :] % (2 * (count + 1))
    angles = jnp.pi * product.astype(jnp.float32) / (count + 1)
    return (math.sqrt(2.0 / (count + 1)) * jnp.sin(angles)).astype(jnp.bfloat16)


def kinetic_phase(count):
    wave = jnp.pi * (jnp.arange(count, dtype=jnp.float32) + 1.0) / (grid_spacing * (count + 1))
    angle_now = time_step * wave * wave / (2.0 * reduced_mass)
    return (jnp.cos(angle_now), jnp.sin(angle_now))


def rotate(real_part, imag_part, cosine, sine_part):
    return (real_part * cosine + imag_part * sine_part, imag_part * cosine - real_part * sine_part)


def legendre_pair(points, count):

    def advance_degree(degree_index, carry):
        previous, current = carry
        degree = degree_index.astype(points.dtype)
        following = ((2.0 * degree + 1.0) * points * current - degree * previous) / (degree + 1.0)
        return (current, following)

    return lax.fori_loop(1, count, advance_degree, (jnp.ones_like(points), points))


def legendre_table(count):
    counter = jnp.arange(count, dtype=jnp.float32)
    points = jnp.cos(jnp.pi * (counter + 0.75) / (count + 0.5))
    for newton_round in range(8):
        previous, current = legendre_pair(points, count)
        slope = count * (points * current - previous) / (points * points - 1.0)
        points = points - current / slope
    previous, current = legendre_pair(points, count)
    slope = count * (points * current - previous) / (points * points - 1.0)
    weights = 2.0 / ((1.0 - points * points) * slope * slope)

    def emit_row(carry, degree_index):
        lower, upper = carry
        degree = degree_index.astype(points.dtype) + 1.0
        following = ((2.0 * degree + 1.0) * points * upper - degree * lower) / (degree + 1.0)
        return ((upper, following), lower)

    carry_end, stacked = lax.scan(
        emit_row, (jnp.ones_like(points), points), jnp.arange(count, dtype=jnp.int32)
    )
    scale = jnp.sqrt(counter + 0.5)[:, None] * jnp.sqrt(weights)[None, :]
    return (stacked * scale).astype(jnp.bfloat16)


def inverse_moment(indices):
    position = grid_spacing * (indices.astype(jnp.float32) + 1.0)
    return 1.0 / (2.0 * reduced_mass * position * position)


def absorber_keep(region, strength):
    marks = (region[..., None] == jnp.arange(NREGION, dtype=jnp.int32)).astype(jnp.float32)
    strength_cell = jnp.sum(marks * strength, axis=-1)
    ramp = (jnp.arange(RABS, dtype=jnp.float32) + 1.0) / RABS
    return jnp.exp(-time_step * strength_cell[..., None] * ramp * ramp)


def finish(new_real, new_imag, keep):
    inner = NS - RABS
    window_real = new_real[..., inner:]
    window_imag = new_imag[..., inner:]
    absorbed = jnp.stack([(1.0 - keep) * window_real, (1.0 - keep) * window_imag])
    state_real = jnp.concatenate([new_real[..., :inner], keep * window_real], axis=-1)
    state_imag = jnp.concatenate([new_imag[..., :inner], keep * window_imag], axis=-1)
    return (jnp.stack([state_real, state_imag]), absorbed)


def route_flux(absorbed, route_owner, route_row, route_weight):
    blocks = absorbed.transpose(1, 2, 0, 3).reshape(-1, 2 * RABS)
    owners = route_owner.reshape(-1)
    targets = route_row.reshape(-1)
    weights = route_weight.reshape(-1)
    pen_count = lax.axis_size("pen")
    capacity = 4 * blocks.shape[0] // pen_count
    entries = jnp.repeat(blocks, 2, axis=0) * weights[:, None]
    marks = (owners[:, None] == jnp.arange(pen_count, dtype=jnp.int32)[None, :]).astype(jnp.int32)
    before = jnp.cumsum(marks, axis=0) - marks
    slots = jnp.sum(before * marks, axis=1)
    send_data = (
        jnp.zeros((pen_count, capacity, 2 * RABS), jnp.float32).at[owners, slots].add(entries)
    )
    send_rows = jnp.zeros((pen_count, capacity), jnp.int32).at[owners, slots].set(targets)
    got_data, got_rows = (
        lax.all_to_all(
            send_data.astype(jnp.bfloat16), "pen", split_axis=0, concat_axis=0, tiled=True
        ).astype(send_data.dtype),
        lax.all_to_all(send_rows, "pen", split_axis=0, concat_axis=0, tiled=True),
    )
    picker = (got_rows.reshape(-1)[None, :] == jnp.arange(PSROWS, dtype=jnp.int32)[:, None]).astype(
        jnp.float32
    )
    return jnp.dot(picker, got_data.reshape(-1, 2 * RABS), precision=lax.Precision.HIGHEST)


def on_device(
    psi, potential, absorber_region, absorber_strength, route_owner, route_row, route_weight
):
    rows_here = psi.shape[1]
    table_short = sine_table(NS)
    table_long = sine_table(NL)
    angular = legendre_table(NANG)
    short_cos, short_sin = kinetic_phase(NS)
    long_cos, long_sin = kinetic_phase(NL)
    order_values = jnp.arange(NANG, dtype=jnp.float32)
    rotor = order_values * (order_values + 1.0)
    half_cos = jnp.cos(0.5 * time_step * potential)
    half_sin = jnp.sin(0.5 * time_step * potential)
    keep = absorber_keep(absorber_region, absorber_strength)
    long_first = lax.axis_index("pen") * rows_here
    long_index = long_first + jnp.arange(rows_here, dtype=jnp.int32)
    state = psi
    flux = jnp.zeros((PSROWS, 2 * RABS), jnp.float32)
    for section_index in range(STEPS):
        first_real, first_imag = rotate(state[0], state[1], half_cos, half_sin)
        moved = jnp.stack([first_real, first_imag]).astype(jnp.bfloat16)
        coeff = jnp.dot(
            moved.reshape(-1, NS), table_short, preferred_element_type=jnp.float32
        ).reshape(moved.shape)
        turn_real, turn_imag = rotate(coeff[0], coeff[1], short_cos, short_sin)
        scaled = jnp.stack([turn_real, turn_imag]).astype(jnp.bfloat16)
        short_done = jnp.dot(
            scaled.reshape(-1, NS), table_short, preferred_element_type=jnp.float32
        )
        short_done = short_done.reshape(moved.shape).astype(jnp.bfloat16)
        long_coeff = jnp.einsum(
            "mn,cnax->cmax",
            table_long,
            lax.all_to_all(short_done, "pen", split_axis=3, concat_axis=1, tiled=True),
            preferred_element_type=jnp.float32,
        )
        long_turn_real, long_turn_imag = rotate(
            long_coeff[0], long_coeff[1], long_cos[:, None, None], long_sin[:, None, None]
        )
        long_scaled = jnp.stack([long_turn_real, long_turn_imag]).astype(jnp.bfloat16)
        long_result = jnp.einsum(
            "mn,cnax->cmax", table_long, long_scaled, preferred_element_type=jnp.float32
        )
        long_done = lax.all_to_all(
            long_result.astype(jnp.bfloat16), "pen", split_axis=1, concat_axis=3, tiled=True
        )
        spread = lax.all_to_all(long_done, "grp", split_axis=3, concat_axis=2, tiled=True)
        width_here = spread.shape[3]
        short_index = lax.axis_index("grp") * width_here + jnp.arange(width_here, dtype=jnp.int32)
        angular_coeff = jnp.einsum(
            "ja,crax->crjx", angular, spread, preferred_element_type=jnp.float32
        )
        energy = jnp.minimum(
            rotor[None, :, None]
            * (
                inverse_moment(long_index)[:, None, None]
                + inverse_moment(short_index)[None, None, :]
            ),
            energy_cap,
        )
        angular_turn_real, angular_turn_imag = rotate(
            angular_coeff[0],
            angular_coeff[1],
            jnp.cos(time_step * energy),
            jnp.sin(time_step * energy),
        )
        angular_scaled = jnp.stack([angular_turn_real, angular_turn_imag]).astype(jnp.bfloat16)
        result = jnp.einsum(
            "ja,crjx->crax", angular, angular_scaled, preferred_element_type=jnp.float32
        )
        turned = result.astype(jnp.bfloat16)
        back = lax.all_to_all(turned, "grp", split_axis=2, concat_axis=3, tiled=True)
        widened = back.astype(jnp.float32)
        new_real, new_imag = rotate(widened[0], widened[1], half_cos, half_sin)
        state, absorbed = finish(new_real, new_imag, keep)
        flux = flux + route_flux(absorbed, route_owner, route_row, route_weight)
    return (state, flux.reshape(1, 1, PSROWS, 2 * RABS))


def solution(mesh):
    return jax.shard_map(
        on_device,
        mesh=mesh,
        in_specs=(
            P(None, "pen", "grp", None),
            P("pen", "grp", None),
            P("pen", "grp"),
            P(),
            P("grp", "pen", None, None),
            P("grp", "pen", None, None),
            P("grp", "pen", None, None),
        ),
        out_specs=(P(None, "pen", "grp", None), P("grp", "pen", None, None)),
        check_vma=False,
    )
```

profile of v0, /device:TPU:8, one launch (start us, length us, event | category | flops | bytes accessed | tf_op | source)
XLA Modules:
  0.0 1460.9 jit_solution(11945442580505841259)
XLA Ops:
  0.7 17.4 %fusion.56 = (bf16[1,64,32,512]{3,2,1,0:T(8,128)(2,1)S(1)}, bf16[1,64,32,512]{3,2,1,0:T(8,128)(2,1)S(1)}) fusion(f32[2,64,32,512]{3,2,1,0:T(8,128)} %param.27, f32[64,32,512]{2,1,0:T(8,128)} %param.28), kind=kLoop, calls=%fused_computation.100 | loop fusion | flops 9437184 | bytes 16777216 | tf_op jit(solution)/shard_map/stack | solution.py:144
  34.8 15.5 %copy.120 = bf16[2,64,32,512]{1,2,0,3:T(8,128)(2,1)} copy(bf16[2,64,32,512]{3,2,1,0:T(8,128)(2,1)} %fusion.52) | data formatting | bytes 8388608 | tf_op jit(solution)/shard_map/convert_element_type | solution.py:153
  136.1 12.0 copy.171
  177.9 13.1 copy.122
  206.2 170.2 %while.159 = (s32[]{:T(128)}, f32[128]{0:T(128)S(1)}, f32[128]{0:T(128)S(1)}, f32[128,128]{1,0:T(8,128)S(1)}, s32[128]{0:T(128)S(1)}, /*index=5*/f32[128]{0:T(12...) while((s32[]{:T(128)}, f32[128]{0:T(128)S(1)}, ...), condition=%wide.region_17.18_spmd, body=%wide.region_16.17_spmd.sunk | while | flops 647 | bytes 5329 | solution.py:68
  386.8 16.5 %copy.156 = bf16[2,64,32,8,64]{1,2,0,4,3:T(8,128)(2,1)} copy(bf16[2,64,32,8,64]{4,2,0,1,3:T(8,128)(2,1)} %bitcast.220) | data formatting | bytes 8388608 | tf_op jit(solution)/shard_map/all_to_all | solution.py:167
  425.6 83.2 %all-to-all-done.2 = bf16[4,2,262144]{2,1,0:T(2,128)(2,1)} async-done(((bf16[4,2,262144]{2,1,0:T(2,128)(2,1)}), bf16[4,2,262144]{2,1,0:T(2,128)(2,1)}, u32[]{:S(2)}, u32[]{:S(2)}) %all-to-all-start.2) | async-done | bytes 4194336 | tf_op jit(solution)/shard_map/all_to_all | solution.py:170
  534.9 17.4 %add_convert_fusion.4 = (bf16[1,64,128,128]{2,3,1,0:T(8,128)(2,1)S(1)}, bf16[1,64,128,128]{2,3,1,0:T(8,128)(2,1)S(1)}) fusion(f32[2,64,128,128]{2,3,1,0:T(8,128)S(1)} %convolution_bitcast_fusion.3, f32[64,128]{1,0:T(8,128)S(1)} %broadcast_add_fusion, f32[128]{0:T(128)S(1)} %iota_multiply_fusion), kind=kLoop, calls=%fused_computation.82 | loop fusion | flops 11534336 | bytes 12616192 | tf_op jit(solution)/shard_map/convert.14
  571.3 89.5 %all-to-all-done.3 = bf16[2,64,128,128]{3,1,0,2:T(8,128)(2,1)} async-done(((bf16[2,64,128,128]{3,1,0,2:T(8,128)(2,1)}), bf16[2,64,128,128]{3,1,0,2:T(8,128)(2,1)}, u32[]{:S(2)}, u32[]{:S(2)}) %all-to-all-start.3) | async-done | bytes 4194336 | tf_op jit(solution)/shard_map/all_to_all | solution.py:195
  695.6 17.0 %multiply_subtract_fusion.1 = (f32[64,32,512]{2,1,0:T(8,128)S(1)}, f32[64,32,512]{2,1,0:T(8,128)S(1)}) fusion(f32[64,32,512]{2,1,0:T(8,128)} %squeeze.47, f32[64,32,512]{2,1,0:T(8,128)} %squeeze.48, f32[64,32,512]{2,1,0:T(8,128)} %param.28), kind=kLoop, calls=%fused_computation.78 | loop fusion | flops 7340032 | bytes 20971520 | tf_op jit(solution)/shard_map/sub | solution.py:37
  716.4 16.2 %fusion.61 = (bf16[1,64,32,512]{3,2,1,0:T(8,128)(2,1)S(1)}, bf16[1,64,32,512]{3,2,1,0:T(8,128)(2,1)S(1)}) fusion(f32[64,32,128]{2,1,0:T(8,128)S(1)} %get-tuple-element.944, f32[64,32,384]{2,1,0:T(8,128)S(1)} %slice.130, f32[64,32,128]{2,1,0:T(8,128)S(1)} %get-tuple-element.937, f32[64,32,384]{2,1,0:T(8,128)S(1)} %slice.128, f32[64,32,512]{2,1,0:T(8,128)S(1)} %copy-done), kind=kLoop, calls=%fused_computation.110 | loop fusion | flops 11534336 | bytes 16777216 | tf_op jit(solution)/shard_map/stack | solution.py:144
  749.5 15.5 %copy.133 = bf16[2,64,32,512]{1,2,0,3:T(8,128)(2,1)} copy(bf16[2,64,32,512]{3,2,1,0:T(8,128)(2,1)} %fusion.45) | data formatting | bytes 8388608 | tf_op jit(solution)/shard_map/convert_element_type | solution.py:153
  775.5 53.6 %all_to_all.146 = bf16[8,2,131072]{2,1,0:T(2,128)(2,1)} all-to-all(bf16[8,2,131072]{2,1,0:T(2,128)(2,1)} %reshape.411), channel_id=1, replica_groups=mesh['grp'=4,'pen'=8] {'pen'}, dimensions={0} | all-to-all | bytes 8388608 | tf_op jit(solution)/shard_map/all_to_all | solution.py:157
  881.3 12.9 copy.135
  904.7 53.6 %all_to_all.147 = bf16[8,2,131072]{2,1,0:T(2,128)(2,1)} all-to-all(bf16[8,2,131072]{2,1,0:T(2,128)(2,1)} %reshape.413), channel_id=1, replica_groups=mesh['grp'=4,'pen'=8] {'pen'}, dimensions={0} | all-to-all | bytes 8388608 | tf_op jit(solution)/shard_map/all_to_all | solution.py:167
  968.5 16.5 %copy.158 = bf16[2,64,32,8,64]{1,2,0,4,3:T(8,128)(2,1)} copy(bf16[2,64,32,8,64]{4,2,0,1,3:T(8,128)(2,1)} %bitcast.224) | data formatting | bytes 8388608 | tf_op jit(solution)/shard_map/all_to_all | solution.py:167
  994.6 100.4 %all_to_all.148 = bf16[4,2,262144]{2,1,0:T(2,128)(2,1)} all-to-all(bf16[4,2,262144]{2,1,0:T(2,128)(2,1)} %reshape.415), channel_id=1, replica_groups=mesh['grp'=4,'pen'=8] {'grp'}, dimensions={0} | all-to-all | bytes 8388608 | tf_op jit(solution)/shard_map/all_to_all | solution.py:170
  1121.1 17.4 %add_convert_fusion = (bf16[1,64,128,128]{2,3,1,0:T(8,128)(2,1)S(1)}, bf16[1,64,128,128]{2,3,1,0:T(8,128)(2,1)S(1)}) fusion(f32[2,64,128,128]{2,3,1,0:T(8,128)S(1)} %convolution_bitcast_fusion.2, f32[64,128]{1,0:T(8,128)S(1)} %broadcast_add_fusion, f32[128]{0:T(128)S(1)} %iota_multiply_fusion), kind=kLoop, calls=%fused_computation.70 | loop fusion | flops 11534336 | bytes 12616192 | tf_op jit(solution)/shard_map/convert.4
  1162.2 16.1 %scatter_custom_fusion = s32[8192]{0:T(1024)} fusion(s32[4096]{0:T(1024)S(1)} %broadcast_select_fusion, s32[4096]{0:T(1024)S(1)} %reshape.380, s32[]{:T(128)} %constant.322.clone.1), kind=kCustom, calls=%fused_computation.162 | custom fusion | bytes 32772
  1178.2 65.8 %all-to-all-done.7 = bf16[2,64,128,128]{3,1,0,2:T(8,128)(2,1)} async-done(((bf16[2,64,128,128]{3,1,0,2:T(8,128)(2,1)}), bf16[2,64,128,128]{3,1,0,2:T(8,128)(2,1)}, u32[]{:S(2)}, u32[]{:S(2)}) %all-to-all-start.7) | async-done | bytes 4194336 | tf_op jit(solution)/shard_map/all_to_all | solution.py:195
  1282.3 17.0 %multiply_add_fusion = (f32[64,32,512]{2,1,0:T(8,128)S(1)}, f32[64,32,512]{2,1,0:T(8,128)S(1)}) fusion(f32[64,32,512]{2,1,0:T(8,128)} %squeeze.52, f32[64,32,512]{2,1,0:T(8,128)} %squeeze.51, f32[64,32,512]{2,1,0:T(8,128)} %param.28), kind=kLoop, calls=%fused_computation.67 | loop fusion | flops 7340032 | bytes 20971520 | tf_op jit(solution)/shard_map/add | solution.py:37
  1314.4 29.1 %scatter_custom_fusion.2 = f32[8192,256]{1,0:T(8,128)} fusion(s32[4096]{0:T(1024)S(1)} %broadcast_select_fusion, f32[]{:T(128)} %constant.333.clone.1, f32[4096,256]{1,0:T(8,128)} %reshape.358, f32[4096]{0:T(1024)S(1)} %mul.1299), kind=kCustom, calls=%fused_computation.60 | custom fusion | flops 2097152 | bytes 12599300
  1365.4 28.8 %scatter_custom_fusion.1 = f32[8192,256]{1,0:T(8,128)} fusion(s32[4096]{0:T(1024)S(1)} %broadcast_select_fusion, f32[]{:T(128)} %constant.333.clone.1, f32[4096,256]{1,0:T(8,128)} %reshape.355, f32[4096]{0:T(1024)S(1)} %mul.1299), kind=kCustom, calls=%fused_computation.62 | custom fusion | flops 2097152 | bytes 12599300
  1420.8 36.1 %all-to-all-done.9 = bf16[8,1024,256]{2,1,0:T(8,128)(2,1)} async-done(((bf16[8,1024,256]{2,1,0:T(8,128)(2,1)}), bf16[8,1024,256]{2,1,0:T(8,128)(2,1)}, u32[]{:S(2)}, u32[]{:S(2)}) %all-to-all-start.9) | async-done | bytes 4194336 | tf_op jit(solution)/shard_map/all_to_all | solution.py:113
  (4256 shorter events, 629.9 us)
Async XLA Ops:
  60.8 64.9 %all-to-all-start = ((bf16[8,2,131072]{2,1,0:T(2,128)(2,1)}), bf16[8,2,131072]{2,1,0:T(2,128)(2,1)}, u32[]{:S(2)}, u32[]{:S(2)}) async-start(bf16[8,2,131072]{2,1,0:T(2,128)(2,1)} %reshape.405), calls=%async_computation | async-start | bytes 8388608 | tf_op jit(solution)/shard_map/all_to_all | solution.py:157
  201.6 174.9 %all-to-all-start.1 = ((bf16[8,2,131072]{2,1,0:T(2,128)(2,1)}), bf16[8,2,131072]{2,1,0:T(2,128)(2,1)}, u32[]{:S(2)}, u32[]{:S(2)}) async-start(bf16[8,2,131072]{2,1,0:T(2,128)(2,1)} %reshape.407), calls=%async_computation.1 | async-start | bytes 8388608 | tf_op jit(solution)/shard_map/all_to_all | solution.py:167
  412.8 96.0 %all-to-all-start.2 = ((bf16[4,2,262144]{2,1,0:T(2,128)(2,1)}), bf16[4,2,262144]{2,1,0:T(2,128)(2,1)}, u32[]{:S(2)}, u32[]{:S(2)}) async-start(bf16[4,2,262144]{2,1,0:T(2,128)(2,1)} %reshape.409), calls=%async_computation.2 | async-start | bytes 8388608 | tf_op jit(solution)/shard_map/all_to_all | solution.py:170
  562.1 9.0 copy-start.10
  562.1 9.0 copy-start.11
  562.1 98.7 %all-to-all-start.3 = ((bf16[2,64,128,128]{3,1,0,2:T(8,128)(2,1)}), bf16[2,64,128,128]{3,1,0,2:T(8,128)(2,1)}, u32[]{:S(2)}, u32[]{:S(2)}) async-start(bf16[2,64,128,128]{3,1,0,2:T(8,128)(2,1)} %copy.128), calls=%async_computation.3 | async-start | bytes 8388608 | tf_op jit(solution)/shard_map/all_to_all | solution.py:195
  713.5 2.9 copy-start
  1148.3 6.8 copy-start.7
  1148.4 95.7 %all-to-all-start.7 = ((bf16[2,64,128,128]{3,1,0,2:T(8,128)(2,1)}), bf16[2,64,128,128]{3,1,0,2:T(8,128)(2,1)}, u32[]{:S(2)}, u32[]{:S(2)}) async-start(bf16[2,64,128,128]{3,1,0,2:T(8,128)(2,1)} %copy.141), calls=%async_computation.7 | async-start | bytes 8388608 | tf_op jit(solution)/shard_map/all_to_all | solution.py:195
  1155.1 4.8 copy-start.8
  1155.1 5.6 copy-start.9
  1155.5 6.4 copy-start.13
  1155.5 6.5 copy-start.12
  1244.0 105.2 %all-to-all-start.8 = ((s32[8,1,1024]{2,1,0:T(1,128)}), s32[8,1,1024]{2,1,0:T(1,128)S(1)}, u32[]{:S(2)}, u32[]{:S(2)}) async-start(s32[8,1,1024]{2,1,0:T(1,128)} %bitcast.53), calls=%async_computation.8 | async-start | bytes 65536 | tf_op jit(solution)/shard_map/all_to_all | solution.py:116
  1299.3 2.0 copy-start.1
  1299.4 3.8 copy-start.3
  1349.2 4.8 copy-start.4
  1349.2 4.8 copy-start.5
  1349.2 53.9 %all-to-all-start.10 = ((bf16[8,1024,256]{2,1,0:T(8,128)(2,1)}), bf16[8,1024,256]{2,1,0:T(8,128)(2,1)}, u32[]{:S(2)}, u32[]{:S(2)}) async-start(bf16[8,1024,256]{2,1,0:T(8,128)(2,1)} %bitcast.228), calls=%async_computation.10 | async-start | bytes 8388608 | tf_op jit(solution)/shard_map/all_to_all | solution.py:113
  1403.2 53.8 %all-to-all-start.9 = ((bf16[8,1024,256]{2,1,0:T(8,128)(2,1)}), bf16[8,1024,256]{2,1,0:T(8,128)(2,1)}, u32[]{:S(2)}, u32[]{:S(2)}) async-start(bf16[8,1024,256]{2,1,0:T(8,128)(2,1)} %bitcast.229), calls=%async_computation.9 | async-start | bytes 8388608 | tf_op jit(solution)/shard_map/all_to_all | solution.py:113
  1408.1 3.1 copy-start.2
  1411.2 1.2 copy-start.6
where the time goes:
time: 1480 us; the launch traced here: 1460 us
  local copies, waits for them, and re-layouts  509 us (34%)
  waiting for transfers between devices  278 us (19%)
  other arithmetic  209 us (14%)
  blocking collectives  208 us (14%)
  loops' own time  135 us (9%)
  matrix products  76 us (5%)
  starting transfers between devices  43.6 us (3%)
    all_to_all x2, waiting for transfers between devices, on_device(): lax.all_to_all(turned, 'grp', split_axis=2, concat_axis=3, tiled=True)  155 us
    unnamed x55, local copies, waits for them, and re-layouts  143 us
    all_to_all x1, blocking collectives, on_device(): lax.all_to_all(long_done, 'grp', split_axis=3, concat_axis=2, tiled=True)  100 us
    another operation x1, loops' own time, legendre_table(): lax.scan(emit_row, (jnp.ones_like(points), points), jnp.arange(count, dty...  88.8 us
    all_to_all x1, waiting for transfers between devices, on_device(): lax.all_to_all(long_done, 'grp', split_axis=3, concat_axis=2, tiled=True)  83.2 us
    dynamic_slice x128, local copies, waits for them, and re-layouts, legendre_table(): lax.scan(emit_row, (jnp.ones_like(points), points), jnp.arange(count, dty...  75.3 us
    unnamed x6, other arithmetic  58.3 us
    all_to_all x1, blocking collectives, on_device(): lax.all_to_all(short_done, 'pen', split_axis=3, concat_axis=1, tiled=True)  53.6 us

commit v1 on v0

--- a/solution.py
+++ b/solution.py
@@ -1,8 +1,13 @@
+import functools
 import math
 
 import jax
 import jax.numpy as jnp
+import ml_dtypes
+import numpy as np
 from jax import lax
+from jax.experimental import pallas as pl
+from jax.experimental.pallas import tpu as pltpu
 from jax.sharding import PartitionSpec as P
 
 NS = 512
@@ -200,9 +205,394 @@
     return (state, flux.reshape(1, 1, PSROWS, 2 * RABS))
 
 
+ROWS = 16
+LANES = 128
+VMEM = 56 * 1024 * 1024
+MESH = pl.DeviceIdType.MESH
+
+
+def tiles_fit(groups, pens):
+    devices = groups * pens
+    return (
+        NL % (devices * ROWS) == 0
+        and NANG % (groups * 32) == 0
+        and NANG % devices == 0
+        and NS % LANES == 0
+        and RABS % LANES == 0
+    )
+
+
+def sine_constant(count):
+    counter = np.arange(count, dtype=np.int64) + 1
+    product = counter[:, None] * counter[None, :] % (2 * (count + 1))
+    table = math.sqrt(2.0 / (count + 1)) * np.sin(np.pi * product / (count + 1))
+    return table.astype(np.float32).astype(ml_dtypes.bfloat16)
+
+
+def phase_constant(count):
+    wave = np.pi * (np.arange(count) + 1.0) / (grid_spacing * (count + 1))
+    turn = time_step * wave * wave / (2.0 * reduced_mass)
+    return np.stack([np.cos(turn), np.sin(turn)]).astype(np.float32)
+
+
+def legendre_constant(count):
+    points = np.cos(np.pi * (np.arange(count) + 0.75) / (count + 0.5))
+
+    def ladder(at):
+        rows = [np.ones_like(at), at]
+        for degree in range(1, count):
+            rows.append(((2.0 * degree + 1.0) * at * rows[-1] - degree * rows[-2]) / (degree + 1.0))
+        return rows
+
+    def slope_of(at, rows):
+        return count * (at * rows[count] - rows[count - 1]) / (at * at - 1.0)
+
+    for newton_round in range(8):
+        rows = ladder(points)
+        points = points - rows[count] / slope_of(points, rows)
+    rows = ladder(points)
+    weights = 2.0 / ((1.0 - points * points) * slope_of(points, rows) ** 2)
+    table = np.sqrt(np.arange(count) + 0.5)[:, None] * np.sqrt(weights)[None, :] * np.stack(rows[:count])
+    return table.astype(np.float32).astype(ml_dtypes.bfloat16)
+
+
+def small_turn(potential):
+    x = (0.5 * time_step) * potential
+    q = x * x
+    cosine = 1.0 + q * (-1.0 / 2 + q * (1.0 / 24 + q * (-1.0 / 720 + q * (1.0 / 40320))))
+    sine = x * (1.0 + q * (-1.0 / 6 + q * (1.0 / 120 + q * (-1.0 / 5040 + q * (1.0 / 362880)))))
+    return cosine, sine
+
+
+def wide_turn(angle):
+    turns = angle * (0.5 / math.pi)
+    half = (turns - jnp.round(turns)) * math.pi
+    q = half * half
+    c = 1.0 + q * (
+        -1.0 / 2
+        + q * (1.0 / 24 + q * (-1.0 / 720 + q * (1.0 / 40320 + q * (-1.0 / 3628800 + q / 479001600.0))))
+    )
+    s = half * (
+        1.0
+        + q * (-1.0 / 6 + q * (1.0 / 120 + q * (-1.0 / 5040 + q * (1.0 / 362880 - q / 39916800.0))))
+    )
+    return 1.0 - 2.0 * s * s, 2.0 * s * c
+
+
+def short_kernel(first, last, *refs):
+    refs = list(refs)
+    wave_ref, pot_ref = refs.pop(0), refs.pop(0)
+    keep_ref = None if first else refs.pop(0)
+    if not last:
+        table_ref, phase_ref = refs.pop(0), refs.pop(0)
+    psi_ref = refs.pop(0) if last else None
+    lost_ref = None if first else refs.pop(0)
+    if not last:
+        out_ref, stage = refs.pop(0), refs.pop(0)
+    angles = pot_ref.shape[1]
+    inner = NS - RABS
+    batch = 4
+
+    def rows(h, carry):
+        parts_real, parts_imag = [], []
+        for k in range(batch):
+            r = h * batch + k
+            half_cos, half_sin = small_turn(pot_ref[r])
+            if first:
+                real, imag = wave_ref[0, r], wave_ref[1, r]
+            else:
+                real = wave_ref[r, 0].astype(jnp.float32)
+                imag = wave_ref[r, 1].astype(jnp.float32)
+                real, imag = rotate(real, imag, half_cos, half_sin)
+                keep = keep_ref[r]
+                tail_real, tail_imag = real[:, inner:], imag[:, inner:]
+                kept_real, kept_imag = keep * tail_real, keep * tail_imag
+                lost_ref[r, :, :RABS] = (tail_real - kept_real).astype(jnp.bfloat16)
+                lost_ref[r, :, RABS:] = (tail_imag - kept_imag).astype(jnp.bfloat16)
+                real = jnp.concatenate([real[:, :inner], kept_real], axis=-1)
+                imag = jnp.concatenate([imag[:, :inner], kept_imag], axis=-1)
+            if last:
+                psi_ref[0, r] = real
+                psi_ref[1, r] = imag
+            else:
+                real, imag = rotate(real, imag, half_cos, half_sin)
+                parts_real.append(real.astype(jnp.bfloat16))
+                parts_imag.append(imag.astype(jnp.bfloat16))
+        if not last:
+            lines = batch * angles
+            both = jnp.concatenate(parts_real + parts_imag, axis=0)
+            coeff = jnp.dot(both, table_ref[...], preferred_element_type=jnp.float32)
+            real, imag = rotate(coeff[:lines], coeff[lines:], phase_ref[0:1], phase_ref[1:2])
+            both = jnp.concatenate([real.astype(jnp.bfloat16), imag.astype(jnp.bfloat16)], axis=0)
+            done = jnp.dot(both, table_ref[...], preferred_element_type=jnp.float32)
+            for q in range(NS // LANES):
+                at = pl.ds(pl.multiple_of(h * lines, lines), lines)
+                stage[0, q, at, :] = done[:lines, q * LANES : (q + 1) * LANES]
+                stage[1, q, at, :] = done[lines:, q * LANES : (q + 1) * LANES]
+        return carry
+
+    lax.fori_loop(0, ROWS // batch, rows, 0)
+    if not last:
+        for a in range(angles):
+            for c in range(2):
+                for q in range(NS // LANES):
+                    picked = stage[c, q, pl.ds(a, ROWS, stride=angles), :]
+                    out_ref[a, c, :, q * LANES : (q + 1) * LANES] = picked.astype(jnp.bfloat16)
+
+
+def short_pass(first, last, wave, potential, keep, table, phase):
+    here, angles = potential.shape[:2]
+    if first:
+        wave_spec = pl.BlockSpec((2, ROWS, angles, NS), lambda i: (0, i, 0, 0))
+    else:
+        wave_spec = pl.BlockSpec((ROWS, 2, angles, NS), lambda i: (i, 0, 0, 0))
+    ins = [wave, potential]
+    in_specs = [wave_spec, pl.BlockSpec((ROWS, angles, NS), lambda i: (i, 0, 0))]
+    outs, out_specs, scratch = [], [], []
+    if not first:
+        ins.append(keep)
+        in_specs.append(pl.BlockSpec((ROWS, angles, RABS), lambda i: (i, 0, 0)))
+    if last:
+        outs.append(jax.ShapeDtypeStruct((2, here, angles, NS), jnp.float32))
+        out_specs.append(pl.BlockSpec((2, ROWS, angles, NS), lambda i: (0, i, 0, 0)))
+    else:
+        ins += [table, phase]
+        in_specs += [
+            pl.BlockSpec((NS, NS), lambda i: (0, 0)),
+            pl.BlockSpec((2, NS), lambda i: (0, 0)),
+        ]
+    if not first:
+        outs.append(jax.ShapeDtypeStruct((here, angles, 2 * RABS), jnp.bfloat16))
+        out_specs.append(pl.BlockSpec((ROWS, angles, 2 * RABS), lambda i: (i, 0, 0)))
+    if not last:
+        outs.append(jax.ShapeDtypeStruct((angles, 2, here, NS), jnp.bfloat16))
+        out_specs.append(pl.BlockSpec((angles, 2, ROWS, NS), lambda i: (0, 0, i, 0)))
+        scratch.append(pltpu.VMEM((2, NS // LANES, ROWS * angles, LANES), jnp.float32))
+    return pl.pallas_call(
+        functools.partial(short_kernel, first, last),
+        grid=(here // ROWS,),
+        in_specs=in_specs,
+        out_specs=out_specs,
+        out_shape=outs,
+        scratch_shapes=scratch,
+        compiler_params=pltpu.CompilerParams(vmem_limit_bytes=VMEM),
+        name="short_first" if first else "short_last" if last else "short_mid",
+    )(*ins)
+
+
+def long_kernel(groups, pens, wave_ref, table_ref, cos_ref, sin_ref, out_ref):
+    table = table_ref[...]
+    tile = 2 * LANES
+    rows = out_ref.shape[4]
+
+    def columns(q, carry):
+        at = pl.ds(pl.multiple_of(q * tile, tile), tile)
+        coeff = [
+            jnp.dot(
+                table,
+                wave_ref[:, 0, c, :, at].reshape(NL, tile),
+                preferred_element_type=jnp.float32,
+            )
+            for c in range(2)
+        ]
+        cosine = jnp.concatenate([cos_ref[...]] * 2, axis=1)
+        sine = jnp.concatenate([sin_ref[...]] * 2, axis=1)
+        turned = rotate(coeff[0], coeff[1], cosine, sine)
+        for c in range(2):
+            done = jnp.dot(table, turned[c].astype(jnp.bfloat16), preferred_element_type=jnp.float32)
+            done = done.astype(jnp.bfloat16).reshape(pens, groups, rows, tile)
+            for g in range(groups):
+                out_ref[g, :, 0, c, :, at] = done[:, g]
+        return carry
+
+    lax.fori_loop(0, NS // tile, columns, 0)
+
+
+def long_pass(groups, wave, table, cosine, sine):
+    pens, angles, _, here, _ = wave.shape
+    rows = here // groups
+    return pl.pallas_call(
+        functools.partial(long_kernel, groups, pens),
+        grid=(angles,),
+        in_specs=[
+            pl.BlockSpec((pens, 1, 2, here, NS), lambda i: (0, i, 0, 0, 0)),
+            pl.BlockSpec((NL, NL), lambda i: (0, 0)),
+            pl.BlockSpec((NL, LANES), lambda i: (0, 0)),
+            pl.BlockSpec((NL, LANES), lambda i: (0, 0)),
+        ],
+        out_specs=pl.BlockSpec((groups, pens, 1, 2, rows, NS), lambda i: (0, 0, i, 0, 0, 0)),
+        out_shape=jax.ShapeDtypeStruct((groups, pens, angles, 2, rows, NS), jnp.bfloat16),
+        compiler_params=pltpu.CompilerParams(vmem_limit_bytes=VMEM),
+        name="long_pass",
+    )(wave, table, cosine, sine)
+
+
+def angle_kernel(wave_ref, table_ref, table_t_ref, inv_long_ref, inv_short_ref, rotor_ref, out_ref, stage):
+    rows = out_ref.shape[1]
+    groups, share = out_ref.shape[0], out_ref.shape[3]
+    stage[...] = wave_ref[...].reshape(stage.shape).astype(jnp.float32)
+    rotor = rotor_ref[...]
+
+    def one(r):
+        both = jnp.concatenate(
+            [stage[pl.ds(c * rows + r, NANG, stride=2 * rows), :] for c in range(2)], axis=1
+        ).astype(jnp.bfloat16)
+        coeff = jnp.dot(table_ref[...], both, preferred_element_type=jnp.float32)
+        moment = inv_long_ref[pl.ds(r, 1), :] + inv_short_ref[...]
+        cosine, sine = wide_turn(time_step * jnp.minimum(rotor * moment, energy_cap))
+        real, imag = rotate(coeff[:, :LANES], coeff[:, LANES:], cosine, sine)
+        both = jnp.concatenate([real, imag], axis=1).astype(jnp.bfloat16)
+        done = jnp.dot(table_t_ref[...], both, preferred_element_type=jnp.float32).astype(jnp.bfloat16)
+        for g in range(groups):
+            for c in range(2):
+                out_ref[g, r, c] = done[g * share : (g + 1) * share, c * LANES : (c + 1) * LANES]
+
+    def four(k, carry):
+        for m in range(4):
+            one(k * 4 + m)
+        return carry
+
+    lax.fori_loop(0, rows // 4, four, 0)
+
+
+def angle_pass(groups, wave, table, table_t, inv_long, inv_short, rotor):
+    rows = wave.shape[2]
+    share = NANG // groups
+    return pl.pallas_call(
+        angle_kernel,
+        grid=(NS // LANES,),
+        in_specs=[
+            pl.BlockSpec((NANG, 2, rows, LANES), lambda i: (0, 0, 0, i)),
+            pl.BlockSpec((NANG, NANG), lambda i: (0, 0)),
+            pl.BlockSpec((NANG, NANG), lambda i: (0, 0)),
+            pl.BlockSpec((rows, LANES), lambda i: (0, 0)),
+            pl.BlockSpec((1, LANES), lambda i: (0, i)),
+            pl.BlockSpec((NANG, LANES), lambda i: (0, 0)),
+        ],
+        out_specs=pl.BlockSpec((groups, rows, 2, share, LANES), lambda i: (0, 0, 0, 0, i)),
+        out_shape=jax.ShapeDtypeStruct((groups, rows, 2, share, NS), jnp.bfloat16),
+        scratch_shapes=[pltpu.VMEM((NANG * 2 * rows, LANES), jnp.float32)],
+        compiler_params=pltpu.CompilerParams(vmem_limit_bytes=VMEM),
+        name="angle_pass",
+    )(wave, table, table_t, inv_long, inv_short, rotor)
+
+
+def exchange_kernel(groups, pens, x_ref, o_ref, send_sem, recv_sem, local_sem):
+    g, p = lax.axis_index("grp"), lax.axis_index("pen")
+    wide_g, wide_p = groups > 1, pens > 1
+    count_g, count_p = lax.axis_size("grp"), lax.axis_size("pen")
+    partners = [(dg, dp) for dg in range(groups) for dp in range(pens) if (dg, dp) != (0, 0)]
+    partners.sort(key=lambda q: -((q[0] != 0) + (q[1] != 0)))
+
+    def place(gg, pp):
+        return (gg * pens if wide_g else 0) + (pp if wide_p else 0)
+
+    def target(q):
+        return lax.rem(g + q[0], count_g), lax.rem(p + q[1], count_p)
+
+    barrier = pltpu.get_barrier_semaphore()
+    for q in partners:
+        pl.semaphore_signal(barrier, inc=1, device_id=target(q), device_id_type=MESH)
+    pl.semaphore_wait(barrier, len(partners))
+    me = place(g, p)
+    copies = []
+    for k, q in enumerate(partners):
+        to = target(q)
+        copy = pltpu.make_async_remote_copy(
+            src_ref=x_ref.at[place(*to)],
+            dst_ref=o_ref.at[me],
+            send_sem=send_sem.at[k],
+            recv_sem=recv_sem.at[k],
+            device_id=to,
+            device_id_type=MESH,
+        )
+        copy.start()
+        copies.append(copy)
+    local = pltpu.make_async_copy(x_ref.at[me], o_ref.at[me], local_sem)
+    local.start()
+    local.wait()
+    for copy in copies:
+        copy.wait()
+
+
+def exchange(x, groups, pens, collective_id):
+    count = groups * pens
+    return pl.pallas_call(
+        functools.partial(exchange_kernel, groups, pens),
+        out_shape=jax.ShapeDtypeStruct(x.shape, x.dtype),
+        in_specs=[pl.BlockSpec(memory_space=pl.ANY)],
+        out_specs=pl.BlockSpec(memory_space=pl.ANY),
+        scratch_shapes=[
+            pltpu.SemaphoreType.DMA((count - 1,)),
+            pltpu.SemaphoreType.DMA((count - 1,)),
+            pltpu.SemaphoreType.DMA,
+        ],
+        compiler_params=pltpu.CompilerParams(collective_id=collective_id, has_side_effects=True),
+        name="exchange_%d" % collective_id,
+    )(x)
+
+
+def route_matrix(route_owner, route_row, route_weight, pens):
+    lines = route_owner.shape[2]
+    keys = (route_owner * PSROWS + route_row).reshape(lines, 2)
+    weights = route_weight.reshape(lines, 2)
+    targets = jnp.arange(pens * PSROWS, dtype=jnp.int32)[:, None]
+    total = jnp.zeros((pens * PSROWS, lines), jnp.float32)
+    for k in range(2):
+        total = total + jnp.where(targets == keys[None, :, k], weights[None, :, k], 0.0)
+    return total.astype(jnp.bfloat16)
+
+
+def on_device_tiled(
+    psi, potential, absorber_region, absorber_strength, route_owner, route_row, route_weight
+):
+    groups, pens = lax.axis_size("grp"), lax.axis_size("pen")
+    here, angles = potential.shape[:2]
+    rows = here // groups
+    share = NANG // (groups * pens)
+    table_short = jnp.asarray(sine_constant(NS))
+    table_long = jnp.asarray(sine_constant(NL))
+    angular_np = legendre_constant(NANG)
+    angular, angular_t = jnp.asarray(angular_np), jnp.asarray(angular_np.T)
+    short_phase = jnp.asarray(phase_constant(NS))
+    long_phase = phase_constant(NL)
+    long_cos = jnp.broadcast_to(jnp.asarray(long_phase[0])[:, None], (NL, LANES))
+    long_sin = jnp.broadcast_to(jnp.asarray(long_phase[1])[:, None], (NL, LANES))
+    order = jnp.arange(NANG, dtype=jnp.float32)
+    rotor = jnp.broadcast_to((order * (order + 1.0))[:, None], (NANG, LANES))
+    first_row = lax.axis_index("pen") * here + lax.axis_index("grp") * rows
+    inv_long = inverse_moment(first_row + jnp.arange(rows, dtype=jnp.int32))
+    inv_long = jnp.broadcast_to(inv_long[:, None], (rows, LANES))
+    inv_short = inverse_moment(jnp.arange(NS, dtype=jnp.int32))[None, :]
+    keep = absorber_keep(absorber_region, absorber_strength)
+    routes = route_matrix(route_owner, route_row, route_weight, pens)
+
+    flux = jnp.zeros((pens * PSROWS, 2 * RABS), jnp.float32)
+    (wave,) = short_pass(True, False, psi, potential, keep, table_short, short_phase)
+    for step in range(STEPS):
+        wave = exchange(wave.reshape(pens, share, 2, here, NS), 1, pens, 1)
+        wave = long_pass(groups, wave, table_long, long_cos, long_sin)
+        wave = exchange(wave.reshape(groups * pens, share, 2, rows, NS), groups, pens, 2)
+        wave = angle_pass(
+            groups, wave.reshape(NANG, 2, rows, NS), angular, angular_t, inv_long, inv_short, rotor
+        )
+        wave = exchange(wave, groups, 1, 3).reshape(here, 2, angles, NS)
+        if step + 1 < STEPS:
+            lost, wave = short_pass(False, False, wave, potential, keep, table_short, short_phase)
+        else:
+            state, lost = short_pass(False, True, wave, potential, keep, table_short, short_phase)
+        flux = flux + jnp.dot(
+            routes, lost.reshape(here * angles, 2 * RABS), preferred_element_type=jnp.float32
+        )
+    parts = lax.all_to_all(flux.reshape(pens, PSROWS, 2 * RABS), "pen", 0, 0, tiled=True)
+    return (state, jnp.sum(parts, axis=0).reshape(1, 1, PSROWS, 2 * RABS))
+
+
 def solution(mesh):
+    groups, pens = mesh.shape["grp"], mesh.shape["pen"]
+    body = on_device_tiled if tiles_fit(groups, pens) else on_device
     return jax.shard_map(
-        on_device,
+        body,
         mesh=mesh,
         in_specs=(
             P(None, "pen", "grp", None),

time: 1480 us -> 605 us (0.41); the launches traced: 1460 us -> 604 us
  Pallas kernels: 0 us -> 582 us
  local copies, waits for them, and re-layouts: 509 us -> 3.21 us
  waiting for transfers between devices: 278 us -> 0 us
  other arithmetic: 209 us -> 2.74 us
  blocking collectives: 208 us -> 12.2 us
  loops' own time: 135 us -> 0 us
  matrix products: 76 us -> 3.34 us
  starting transfers between devices: 43.6 us -> 0 us
    pallas_call x0 -> x13, Pallas kernels: none -> 582 us  [the longest x6 479 us: exchange(): pl.pallas_call(functools.partial(exchange_kernel, groups, pens), out_shap...]
    all_to_all x8 -> x0, waiting for transfers between devices: 278 us -> none  [the longest x2 155 us: on_device(): lax.all_to_all(turned, 'grp', split_axis=2, concat_axis=3, tiled=True)]
    all_to_all x3 -> x1, blocking collectives: 208 us -> 12.2 us  [on_device_tiled(): lax.all_to_all(flux.reshape(pens, PSROWS, 2 * RABS), 'pen', 0, 0, tiled=T...]
    unnamed x55 -> x16, local copies, waits for them, and re-layouts: 143 us -> 0.04 us
    another operation x10 -> x0, loops' own time: 135 us -> none  [the longest x1 88.8 us: legendre_table(): lax.scan(emit_row, (jnp.ones_like(points), points), jnp.arange(count, dty...]
    all_to_all x12 -> x0, local copies, waits for them, and re-layouts: 122 us -> none  [the longest x4 48 us: on_device(): lax.all_to_all(short_done, 'pen', split_axis=3, concat_axis=1, tiled=True)]
    another operation x17 -> x0, other arithmetic: 86.6 us -> none
    dynamic_slice x128 -> x0, local copies, waits for them, and re-layouts: 75.3 us -> none  [legendre_table(): lax.scan(emit_row, (jnp.ones_like(points), points), jnp.arange(count, dty...]
where the time goes in v1:
time: 605 us; the launch traced here: 604 us
  Pallas kernels  582 us (96%)
  blocking collectives  12.2 us (2%)
    pallas_call x6, Pallas kernels, exchange(): pl.pallas_call(functools.partial(exchange_kernel, groups, pens), out_shap...  479 us
    pallas_call x3, Pallas kernels, short_pass(): pl.pallas_call(functools.partial(short_kernel, first, last), grid=(here /...  52.2 us
    pallas_call x2, Pallas kernels, angle_pass(): pl.pallas_call(angle_kernel, grid=(NS // LANES,), in_specs=[pl.BlockSpec(...  32.1 us
    pallas_call x2, Pallas kernels, long_pass(): pl.pallas_call(functools.partial(long_kernel, groups, pens), grid=(angles...  18.2 us
    all_to_all x1, blocking collectives, on_device_tiled(): lax.all_to_all(flux.reshape(pens, PSROWS, 2 * RABS), 'pen', 0, 0, tiled=T...  12.2 us

profile of v1, /device:TPU:8, one launch (start us, length us, event | category | flops | bytes accessed | tf_op | source)
XLA Modules:
  0.0 604.2 jit_solution(17469102833615398039)
XLA Ops:
  0.6 0.6 multiply_divide_fusion.inv_short_ref
  1.3 20.4 %short_first.1 = bf16[32,2,64,512]{3,2,1,0:T(8,128)(2,1)} custom-call(f32[2,64,32,512]{3,2,1,0:T(8,128)} %refs_0_.1, f32[64,32,512]{2,1,0:T(8,128)} %refs_1_.5, bf16[512,512]{1,0:T(8,128)(2,1)} %constant.45.clone.refs_2_.table_ref.refs_3_, f32[2,512]{1,0:T(2,128)} %constant.48.clone.refs_3_.refs_4_), custom_call_target="tpu_custom_call" | custom-call | tf_op jit(solution)/shard_map/short_first/pallas_call | solution.py:371
  21.7 48.4 %exchange_1.2.wave_ref = bf16[8,4,2,64,512]{4,3,2,1,0:T(8,128)(2,1)} custom-call(bf16[8,4,2,64,512]{4,3,2,1,0:T(8,128)(2,1)} %bitcast.21), custom_call_target="tpu_custom_call" | custom-call | tf_op jit(solution)/shard_map/exchange_1/pallas_call | solution.py:520
  70.1 0.8 broadcast_in_dim.56.cos_ref
  70.9 0.9 broadcast_in_dim.57.sin_ref
  71.8 9.1 %long_pass.2 = bf16[4,8,4,2,16,512]{5,4,3,2,1,0:T(8,128)(2,1)} custom-call(bf16[8,4,2,64,512]{4,3,2,1,0:T(8,128)(2,1)} %exchange_1.2.wave_ref, bf16[512,512]{1,0:T(8,128)(2,1)} %constant.45.clone.refs_2_.table_ref.refs_3_, f32[512,128]{1,0:T(8,128)} %broadcast_in_dim.56.cos_ref, f32[512,128]{1,0:T(8,128)} %broadcast_in_dim.57.sin_ref), custom_call_target="tpu_custom_call" | custom-call | tf_op jit(solution)/shard_map/long_pass/pallas_call | solution.py:414
  80.9 98.7 %exchange_2.2 = bf16[32,4,2,16,512]{4,3,2,1,0:T(8,128)(2,1)} custom-call(bf16[32,4,2,16,512]{4,3,2,1,0:T(8,128)(2,1)} %bitcast.27), custom_call_target="tpu_custom_call" | custom-call | tf_op jit(solution)/shard_map/exchange_2/pallas_call | solution.py:520
  179.6 0.7 broadcast_in_dim.58.inv_long_ref
  180.3 0.7 broadcast_in_dim.59.rotor_ref
  181.0 16.1 %angle_pass.2.x_ref = bf16[4,16,2,32,512]{4,3,2,1,0:T(8,128)(2,1)} custom-call(bf16[128,2,16,512]{3,2,1,0:T(8,128)(2,1)} %bitcast.24, bf16[128,128]{1,0:T(8,128)(2,1)} %constant.46.clone.table_ref, bf16[128,128]{1,0:T(8,128)(2,1)} %constant.47.clone.table_t_ref, f32[16,128]{1,0:T(8,128)} %broadcast_in_dim.58.inv_long_ref, ...), custom_call_target="tpu_custom_call" | custom-call | tf_op jit(solution)/shard_map/angle_pass/pallas_call | solution.py:461
  197.1 93.6 %exchange_3.2 = bf16[4,16,2,32,512]{4,3,2,1,0:T(8,128)(2,1)} custom-call(bf16[4,16,2,32,512]{4,3,2,1,0:T(8,128)(2,1)} %angle_pass.2.x_ref), custom_call_target="tpu_custom_call" | custom-call | tf_op jit(solution)/shard_map/exchange_3/pallas_call | solution.py:520
  290.8 0.1 copy.17
  290.9 1.4 multiply_exponential_fusion.refs_2_
  292.2 22.2 %short_mid.1 = (bf16[64,32,256]{2,1,0:T(8,128)(2,1)}, bf16[32,2,64,512]{3,2,1,0:T(8,128)(2,1)}) custom-call(bf16[64,2,32,512]{3,2,1,0:T(8,128)(2,1)} %bitcast.22, f32[64,32,512]{2,1,0:T(8,128)} %refs_1_.5, f32[64,32,128]{2,1,0:T(8,128)} %multiply_exponential_fusion.refs_2_, bf16[512,512]{1,0:T(8,128)(2,1)} %constant.45.clone.refs_2_.table_ref.refs_3_, ...), custom_call_target="tpu_custom_call" | custom-call | tf_op jit(solution)/shard_map/short_mid/pallas_call | solution.py:371
  314.5 46.5 %exchange_1.3.wave_ref = bf16[8,4,2,64,512]{4,3,2,1,0:T(8,128)(2,1)} custom-call(bf16[8,4,2,64,512]{4,3,2,1,0:T(8,128)(2,1)} %bitcast.28), custom_call_target="tpu_custom_call" | custom-call | tf_op jit(solution)/shard_map/exchange_1/pallas_call | solution.py:520
  361.0 9.1 %long_pass.3 = bf16[4,8,4,2,16,512]{5,4,3,2,1,0:T(8,128)(2,1)} custom-call(bf16[8,4,2,64,512]{4,3,2,1,0:T(8,128)(2,1)} %exchange_1.3.wave_ref, bf16[512,512]{1,0:T(8,128)(2,1)} %constant.45.clone.refs_2_.table_ref.refs_3_, f32[512,128]{1,0:T(8,128)} %broadcast_in_dim.56.cos_ref, f32[512,128]{1,0:T(8,128)} %broadcast_in_dim.57.sin_ref), custom_call_target="tpu_custom_call" | custom-call | tf_op jit(solution)/shard_map/long_pass/pallas_call | solution.py:414
  370.1 98.5 %exchange_2.3 = bf16[32,4,2,16,512]{4,3,2,1,0:T(8,128)(2,1)} custom-call(bf16[32,4,2,16,512]{4,3,2,1,0:T(8,128)(2,1)} %bitcast.25), custom_call_target="tpu_custom_call" | custom-call | tf_op jit(solution)/shard_map/exchange_2/pallas_call | solution.py:520
  468.6 16.1 %angle_pass.3.x_ref = bf16[4,16,2,32,512]{4,3,2,1,0:T(8,128)(2,1)} custom-call(bf16[128,2,16,512]{3,2,1,0:T(8,128)(2,1)} %bitcast.23, bf16[128,128]{1,0:T(8,128)(2,1)} %constant.46.clone.table_ref, bf16[128,128]{1,0:T(8,128)(2,1)} %constant.47.clone.table_t_ref, f32[16,128]{1,0:T(8,128)} %broadcast_in_dim.58.inv_long_ref, ...), custom_call_target="tpu_custom_call" | custom-call | tf_op jit(solution)/shard_map/angle_pass/pallas_call | solution.py:461
  484.7 93.6 %exchange_3.3 = bf16[4,16,2,32,512]{4,3,2,1,0:T(8,128)(2,1)} custom-call(bf16[4,16,2,32,512]{4,3,2,1,0:T(8,128)(2,1)} %angle_pass.3.x_ref), custom_call_target="tpu_custom_call" | custom-call | tf_op jit(solution)/shard_map/exchange_3/pallas_call | solution.py:520
  578.3 9.5 %short_last.1 = (f32[2,64,32,512]{3,2,1,0:T(8,128)}, bf16[64,32,256]{2,1,0:T(8,128)(2,1)}) custom-call(bf16[64,2,32,512]{3,2,1,0:T(8,128)(2,1)} %bitcast.26, f32[64,32,512]{2,1,0:T(8,128)} %refs_1_.5, f32[64,32,128]{2,1,0:T(8,128)} %multiply_exponential_fusion.refs_2_), custom_call_target="tpu_custom_call" | custom-call | tf_op jit(solution)/shard_map/short_last/pallas_call | solution.py:371
  588.0 2.3 fusion
  590.3 1.0 fusion.2
  591.3 12.2 %all_to_all.5 = f32[8,64,256]{2,1,0:T(8,128)S(1)} all-to-all(f32[8,64,256]{2,1,0:T(8,128)S(1)} %bitcast.29), channel_id=1, replica_groups=mesh['grp'=4,'pen'=8] {'pen'}, dimensions={0} | all-to-all | bytes 1048576 | tf_op jit(solution)/shard_map/all_to_all | solution.py:587
  603.6 0.7 reduce_sum.19
  (24 shorter events, 0.2 us)
Async XLA Ops:
  21.7 48.4 %copy-start.5 = (f32[512]{0:T(512)S(1)}, f32[512]{0:T(512)}, u32[]{:S(2)}) copy-start(f32[512]{0:T(512)} %constant.49.clone) | copy-start | bytes 6148
  21.7 49.3 %copy-start.4 = (f32[512]{0:T(512)S(1)}, f32[512]{0:T(512)}, u32[]{:S(2)}) copy-start(f32[512]{0:T(512)} %constant.50.clone) | copy-start | bytes 6148
  197.1 93.6 %copy-start.2 = (s32[64,32]{0,1:T(8,128)S(1)}, s32[64,32]{0,1:T(8,128)}, u32[]{:S(2)}) copy-start(s32[64,32]{0,1:T(8,128)} %param.16) | copy-start | bytes 24580
  197.1 93.6 %copy-start.6 = (f32[4]{0:T(128)S(1)}, f32[4]{0:T(128)}, u32[]{:S(2)}) copy-start(f32[4]{0:T(128)} %param.17) | copy-start | bytes 52
  578.3 9.6 %copy-start = (s32[1,1,2048,2]{2,3,1,0:T(2,128)S(1)}, s32[1,1,2048,2]{2,3,1,0:T(2,128)}, u32[]{:S(2)}) copy-start(s32[1,1,2048,2]{2,3,1,0:T(2,128)} %param.19) | copy-start | bytes 49156
  578.3 9.6 %copy-start.1 = (s32[1,1,2048,2]{2,3,1,0:T(2,128)S(1)}, s32[1,1,2048,2]{2,3,1,0:T(2,128)}, u32[]{:S(2)}) copy-start(s32[1,1,2048,2]{2,3,1,0:T(2,128)} %param.18) | copy-start | bytes 49156
  578.3 9.6 %copy-start.3 = (f32[1,1,2048,2]{2,3,1,0:T(2,128)S(1)}, f32[1,1,2048,2]{2,3,1,0:T(2,128)}, u32[]{:S(2)}) copy-start(f32[1,1,2048,2]{2,3,1,0:T(2,128)} %param.20) | copy-start | bytes 49156
  587.9 2.3 copy-start.7

commit v2 on v1

--- a/solution.py
+++ b/solution.py
@@ -207,6 +207,7 @@
 
 ROWS = 16
 LANES = 128
+PAD = 8
 VMEM = 56 * 1024 * 1024
 MESH = pl.DeviceIdType.MESH
 
@@ -279,7 +280,41 @@
     return 1.0 - 2.0 * s * s, 2.0 * s * c
 
 
-def short_kernel(first, last, *refs):
+def greet(targets):
+    barrier = pltpu.get_barrier_semaphore()
+    for to in targets:
+        pl.semaphore_signal(barrier, inc=1, device_id=to, device_id_type=MESH)
+    pl.semaphore_wait(barrier, len(targets))
+
+
+def chunk_copies(chunk, me, source, landing, targets, spots, send_sem, recv_sem):
+    return [
+        pltpu.make_async_remote_copy(
+            src_ref=source(chunk, spot),
+            dst_ref=landing(chunk, me),
+            send_sem=send_sem.at[chunk, k],
+            recv_sem=recv_sem.at[chunk, k],
+            device_id=to,
+            device_id_type=MESH,
+        )
+        for k, (to, spot) in enumerate(zip(targets, spots))
+    ]
+
+
+def send_chunk(chunk, chunks, me, source, landing, targets, spots, send_sem, recv_sem, local_sem):
+    for copy in chunk_copies(chunk, me, source, landing, targets, spots, send_sem, recv_sem):
+        copy.start()
+    pltpu.make_async_copy(source(chunk, me), landing(chunk, me), local_sem.at[chunk]).start()
+
+    @pl.when(chunk == chunks - 1)
+    def _():
+        for part in range(chunks):
+            for copy in chunk_copies(part, me, source, landing, targets, spots, send_sem, recv_sem):
+                copy.wait()
+            pltpu.make_async_copy(source(part, me), landing(part, me), local_sem.at[part]).wait()
+
+
+def short_kernel(first, last, pens, chunks, *refs):
     refs = list(refs)
     wave_ref, pot_ref = refs.pop(0), refs.pop(0)
     keep_ref = None if first else refs.pop(0)
@@ -288,7 +323,16 @@
     psi_ref = refs.pop(0) if last else None
     lost_ref = None if first else refs.pop(0)
     if not last:
-        out_ref, stage = refs.pop(0), refs.pop(0)
+        out_ref, stage, blocks, send_sem, recv_sem, local_sem = refs
+        chunk = pl.program_id(0)
+        g, p = lax.axis_index("grp"), lax.axis_index("pen")
+        spots = [lax.rem(p + d, pens) for d in range(1, pens)]
+        targets = [(g, spot) for spot in spots]
+
+        @pl.when(chunk == 0)
+        def _():
+            greet(targets)
+
     angles = pot_ref.shape[1]
     inner = NS - RABS
     batch = 4
@@ -325,10 +369,15 @@
             real, imag = rotate(coeff[:lines], coeff[lines:], phase_ref[0:1], phase_ref[1:2])
             both = jnp.concatenate([real.astype(jnp.bfloat16), imag.astype(jnp.bfloat16)], axis=0)
             done = jnp.dot(both, table_ref[...], preferred_element_type=jnp.float32)
-            for q in range(NS // LANES):
-                at = pl.ds(pl.multiple_of(h * lines, lines), lines)
-                stage[0, q, at, :] = done[:lines, q * LANES : (q + 1) * LANES]
-                stage[1, q, at, :] = done[lines:, q * LANES : (q + 1) * LANES]
+            pitch = angles + PAD
+            for k in range(batch):
+                at = pl.ds(pl.multiple_of((h * batch + k) * pitch, 8), angles)
+                for c in range(2):
+                    for q in range(NS // LANES):
+                        first_line = c * lines + k * angles
+                        stage[c, q, at, :] = done[
+                            first_line : first_line + angles, q * LANES : (q + 1) * LANES
+                        ]
         return carry
 
     lax.fori_loop(0, ROWS // batch, rows, 0)
@@ -336,11 +385,25 @@
         for a in range(angles):
             for c in range(2):
                 for q in range(NS // LANES):
-                    picked = stage[c, q, pl.ds(a, ROWS, stride=angles), :]
-                    out_ref[a, c, :, q * LANES : (q + 1) * LANES] = picked.astype(jnp.bfloat16)
-
-
-def short_pass(first, last, wave, potential, keep, table, phase):
+                    picked = stage[c, q, pl.ds(a, ROWS, stride=angles + PAD), :]
+                    to, at = divmod(a, angles // pens)
+                    blocks[chunk, to, at, c, :, q * LANES : (q + 1) * LANES] = picked.astype(
+                        jnp.bfloat16
+                    )
+
+        def source(part, spot):
+            return blocks.at[part, spot]
+
+        def landing(part, spot):
+            start = part * ROWS if isinstance(part, int) else pl.multiple_of(part * ROWS, ROWS)
+            return out_ref.at[spot, :, :, pl.ds(start, ROWS), :]
+
+        send_chunk(
+            chunk, chunks, p, source, landing, targets, spots, send_sem, recv_sem, local_sem
+        )
+
+
+def short_pass(first, last, pens, wave, potential, keep, table, phase):
     here, angles = potential.shape[:2]
     if first:
         wave_spec = pl.BlockSpec((2, ROWS, angles, NS), lambda i: (0, i, 0, 0))
@@ -365,17 +428,26 @@
         outs.append(jax.ShapeDtypeStruct((here, angles, 2 * RABS), jnp.bfloat16))
         out_specs.append(pl.BlockSpec((ROWS, angles, 2 * RABS), lambda i: (i, 0, 0)))
     if not last:
-        outs.append(jax.ShapeDtypeStruct((angles, 2, here, NS), jnp.bfloat16))
-        out_specs.append(pl.BlockSpec((angles, 2, ROWS, NS), lambda i: (0, 0, i, 0)))
-        scratch.append(pltpu.VMEM((2, NS // LANES, ROWS * angles, LANES), jnp.float32))
+        share, chunks = angles // pens, here // ROWS
+        outs.append(jax.ShapeDtypeStruct((pens, share, 2, here, NS), jnp.bfloat16))
+        out_specs.append(pl.BlockSpec(memory_space=pl.ANY))
+        scratch.append(pltpu.VMEM((2, NS // LANES, ROWS * (angles + PAD), LANES), jnp.float32))
+        scratch.append(pltpu.VMEM((chunks, pens, share, 2, ROWS, NS), jnp.bfloat16))
+        scratch.append(pltpu.SemaphoreType.DMA((chunks, pens - 1)))
+        scratch.append(pltpu.SemaphoreType.DMA((chunks, pens - 1)))
+        scratch.append(pltpu.SemaphoreType.DMA((chunks,)))
     return pl.pallas_call(
-        functools.partial(short_kernel, first, last),
+        functools.partial(short_kernel, first, last, pens, here // ROWS),
         grid=(here // ROWS,),
         in_specs=in_specs,
         out_specs=out_specs,
         out_shape=outs,
         scratch_shapes=scratch,
-        compiler_params=pltpu.CompilerParams(vmem_limit_bytes=VMEM),
+        compiler_params=pltpu.CompilerParams(vmem_limit_bytes=VMEM)
+        if last
+        else pltpu.CompilerParams(
+            vmem_limit_bytes=VMEM, collective_id=1 if first else 4, has_side_effects=True
+        ),
         name="short_first" if first else "short_last" if last else "short_mid",
     )(*ins)
 
@@ -427,15 +499,26 @@
     )(wave, table, cosine, sine)
 
 
-def angle_kernel(wave_ref, table_ref, table_t_ref, inv_long_ref, inv_short_ref, rotor_ref, out_ref, stage):
+def angle_kernel(wave_ref, table_ref, table_t_ref, inv_long_ref, inv_short_ref, rotor_ref, out_ref, stage, blocks, send_sem, recv_sem, local_sem):
     rows = out_ref.shape[1]
     groups, share = out_ref.shape[0], out_ref.shape[3]
-    stage[...] = wave_ref[...].reshape(stage.shape).astype(jnp.float32)
+    pitch = 2 * rows + PAD
+    for a in range(NANG):
+        for c in range(2):
+            stage[a * pitch + c * rows : a * pitch + (c + 1) * rows, :] = wave_ref[a, c].astype(jnp.float32)
     rotor = rotor_ref[...]
+    chunk = pl.program_id(0)
+    g, p = lax.axis_index("grp"), lax.axis_index("pen")
+    spots = [lax.rem(g + d, groups) for d in range(1, groups)]
+    targets = [(spot, p) for spot in spots]
+
+    @pl.when(chunk == 0)
+    def _():
+        greet(targets)
 
     def one(r):
         both = jnp.concatenate(
-            [stage[pl.ds(c * rows + r, NANG, stride=2 * rows), :] for c in range(2)], axis=1
+            [stage[pl.ds(c * rows + r, NANG, stride=pitch), :] for c in range(2)], axis=1
         ).astype(jnp.bfloat16)
         coeff = jnp.dot(table_ref[...], both, preferred_element_type=jnp.float32)
         moment = inv_long_ref[pl.ds(r, 1), :] + inv_short_ref[...]
@@ -443,9 +526,11 @@
         real, imag = rotate(coeff[:, :LANES], coeff[:, LANES:], cosine, sine)
         both = jnp.concatenate([real, imag], axis=1).astype(jnp.bfloat16)
         done = jnp.dot(table_t_ref[...], both, preferred_element_type=jnp.float32).astype(jnp.bfloat16)
-        for g in range(groups):
+        for to in range(groups):
             for c in range(2):
-                out_ref[g, r, c] = done[g * share : (g + 1) * share, c * LANES : (c + 1) * LANES]
+                blocks[chunk, to, r, c] = done[
+                    to * share : (to + 1) * share, c * LANES : (c + 1) * LANES
+                ]
 
     def four(k, carry):
         for m in range(4):
@@ -453,6 +538,17 @@
         return carry
 
     lax.fori_loop(0, rows // 4, four, 0)
+
+    def source(part, spot):
+        return blocks.at[part, spot]
+
+    def landing(part, spot):
+        start = part * LANES if isinstance(part, int) else pl.multiple_of(part * LANES, LANES)
+        return out_ref.at[spot, :, :, :, pl.ds(start, LANES)]
+
+    send_chunk(
+        chunk, NS // LANES, g, source, landing, targets, spots, send_sem, recv_sem, local_sem
+    )
 
 
 def angle_pass(groups, wave, table, table_t, inv_long, inv_short, rotor):
@@ -469,10 +565,17 @@
             pl.BlockSpec((1, LANES), lambda i: (0, i)),
             pl.BlockSpec((NANG, LANES), lambda i: (0, 0)),
         ],
-        out_specs=pl.BlockSpec((groups, rows, 2, share, LANES), lambda i: (0, 0, 0, 0, i)),
+        out_specs=pl.BlockSpec(memory_space=pl.ANY),
         out_shape=jax.ShapeDtypeStruct((groups, rows, 2, share, NS), jnp.bfloat16),
-        scratch_shapes=[pltpu.VMEM((NANG * 2 * rows, LANES), jnp.float32)],
-        compiler_params=pltpu.CompilerParams(vmem_limit_bytes=VMEM),
+        scratch_shapes=[pltpu.VMEM((NANG * (2 * rows + PAD), LANES), jnp.float32),
+            pltpu.VMEM((NS // LANES, groups, rows, 2, share, LANES), jnp.bfloat16),
+            pltpu.SemaphoreType.DMA((NS // LANES, groups - 1)),
+            pltpu.SemaphoreType.DMA((NS // LANES, groups - 1)),
+            pltpu.SemaphoreType.DMA((NS // LANES,)),
+        ],
+        compiler_params=pltpu.CompilerParams(
+            vmem_limit_bytes=VMEM, collective_id=3, has_side_effects=True
+        ),
         name="angle_pass",
     )(wave, table, table_t, inv_long, inv_short, rotor)
 
@@ -568,19 +671,18 @@
     routes = route_matrix(route_owner, route_row, route_weight, pens)
 
     flux = jnp.zeros((pens * PSROWS, 2 * RABS), jnp.float32)
-    (wave,) = short_pass(True, False, psi, potential, keep, table_short, short_phase)
+    (wave,) = short_pass(True, False, pens, psi, potential, keep, table_short, short_phase)
     for step in range(STEPS):
-        wave = exchange(wave.reshape(pens, share, 2, here, NS), 1, pens, 1)
         wave = long_pass(groups, wave, table_long, long_cos, long_sin)
         wave = exchange(wave.reshape(groups * pens, share, 2, rows, NS), groups, pens, 2)
         wave = angle_pass(
             groups, wave.reshape(NANG, 2, rows, NS), angular, angular_t, inv_long, inv_short, rotor
         )
-        wave = exchange(wave, groups, 1, 3).reshape(here, 2, angles, NS)
+        wave = wave.reshape(here, 2, angles, NS)
         if step + 1 < STEPS:
-            lost, wave = short_pass(False, False, wave, potential, keep, table_short, short_phase)
+            lost, wave = short_pass(False, False, pens, wave, potential, keep, table_short, short_phase)
         else:
-            state, lost = short_pass(False, True, wave, potential, keep, table_short, short_phase)
+            state, lost = short_pass(False, True, pens, wave, potential, keep, table_short, short_phase)
         flux = flux + jnp.dot(
             routes, lost.reshape(here * angles, 2 * RABS), preferred_element_type=jnp.float32
         )

time: 605 us -> 550 us (0.909)
  Pallas kernels: 582 us -> 527 us
    pallas_call x6 -> x2, Pallas kernels: 479 us -> 198 us  [exchange(): pl.pallas_call(functools.partial(exchange_kernel, groups, pens), out_shap...]
    pallas_call x2, Pallas kernels: 32.1 us -> 195 us  [angle_pass(): pl.pallas_call(angle_kernel, grid=(NS // LANES,), in_specs=[pl.BlockSpec(...]
    pallas_call x3, Pallas kernels: 52.2 us -> 117 us  [short_pass(): pl.pallas_call(functools.partial(short_kernel, first, last, pens, here //...]
where the time goes in v2:
time: 550 us
  Pallas kernels  527 us (96%)
  blocking collectives  12.2 us (2%)
    pallas_call x2, Pallas kernels, exchange(): pl.pallas_call(functools.partial(exchange_kernel, groups, pens), out_shap...  198 us
    pallas_call x2, Pallas kernels, angle_pass(): pl.pallas_call(angle_kernel, grid=(NS // LANES,), in_specs=[pl.BlockSpec(...  195 us
    pallas_call x3, Pallas kernels, short_pass(): pl.pallas_call(functools.partial(short_kernel, first, last, pens, here //...  117 us
    pallas_call x2, Pallas kernels, long_pass(): pl.pallas_call(functools.partial(long_kernel, groups, pens), grid=(angles...  18.2 us
    all_to_all x1, blocking collectives, on_device_tiled(): lax.all_to_all(flux.reshape(pens, PSROWS, 2 * RABS), 'pen', 0, 0, tiled=T...  12.2 us

profile of v2, /device:TPU:8, one launch (start us, length us, event | category | flops | bytes accessed | tf_op | source)
XLA Modules:
  0.0 549.8 jit_solution(9498549456421789545)
XLA Ops:
  0.6 0.6 multiply_divide_fusion.inv_short_ref
  1.3 0.0 copy-start.4
  1.3 53.7 %short_first.1.wave_ref = bf16[8,4,2,64,512]{4,3,2,1,0:T(8,128)(2,1)} custom-call(f32[2,64,32,512]{3,2,1,0:T(8,128)} %refs_0_.1, f32[64,32,512]{2,1,0:T(8,128)} %refs_1_.5, bf16[512,512]{1,0:T(8,128)(2,1)} %constant.45.clone.refs_2_.table_ref.refs_3_, f32[2,512]{1,0:T(2,128)} %constant.48.clone.refs_3_.refs_4_), custom_call_target="tpu_custom_call" | custom-call | tf_op jit(solution)/shard_map/short_first/pallas_call | solution.py:439
  55.0 0.8 broadcast_in_dim.56.cos_ref
  55.8 0.8 broadcast_in_dim.57.sin_ref
  56.7 9.1 %long_pass.2 = bf16[4,8,4,2,16,512]{5,4,3,2,1,0:T(8,128)(2,1)} custom-call(bf16[8,4,2,64,512]{4,3,2,1,0:T(8,128)(2,1)} %short_first.1.wave_ref, bf16[512,512]{1,0:T(8,128)(2,1)} %constant.45.clone.refs_2_.table_ref.refs_3_, f32[512,128]{1,0:T(8,128)} %broadcast_in_dim.56.cos_ref, f32[512,128]{1,0:T(8,128)} %broadcast_in_dim.57.sin_ref), custom_call_target="tpu_custom_call" | custom-call | tf_op jit(solution)/shard_map/long_pass/pallas_call | solution.py:486
  65.8 98.9 %exchange_2.2 = bf16[32,4,2,16,512]{4,3,2,1,0:T(8,128)(2,1)} custom-call(bf16[32,4,2,16,512]{4,3,2,1,0:T(8,128)(2,1)} %bitcast.24), custom_call_target="tpu_custom_call" | custom-call | tf_op jit(solution)/shard_map/exchange_2/pallas_call | solution.py:623
  164.7 0.1 select_reduce_fusion
  164.8 0.1 copy.17
  164.9 1.4 multiply_exponential_fusion.refs_2_
  166.3 0.7 broadcast_in_dim.58.inv_long_ref
  167.0 0.7 broadcast_in_dim.59.rotor_ref
  167.7 97.5 %angle_pass.2 = bf16[4,16,2,32,512]{4,3,2,1,0:T(8,128)(2,1)} custom-call(bf16[128,2,16,512]{3,2,1,0:T(8,128)(2,1)} %bitcast.19, bf16[128,128]{1,0:T(8,128)(2,1)} %constant.46.clone.table_ref, bf16[128,128]{1,0:T(8,128)(2,1)} %constant.47.clone.table_t_ref, f32[16,128]{1,0:T(8,128)} %broadcast_in_dim.58.inv_long_ref, ...), custom_call_target="tpu_custom_call" | custom-call | tf_op jit(solution)/shard_map/angle_pass/pallas_call | solution.py:557
  265.2 53.4 %short_mid.1 = (bf16[64,32,256]{2,1,0:T(8,128)(2,1)}, bf16[8,4,2,64,512]{4,3,2,1,0:T(8,128)(2,1)}) custom-call(bf16[64,2,32,512]{3,2,1,0:T(8,128)(2,1)} %bitcast.22, f32[64,32,512]{2,1,0:T(8,128)} %refs_1_.5, f32[64,32,128]{2,1,0:T(8,128)} %multiply_exponential_fusion.refs_2_, bf16[512,512]{1,0:T(8,128)(2,1)} %constant.45.clone.refs_2_.table_ref.refs_3_, ...), custom_call_target="tpu_custom_call" | custom-call | tf_op jit(solution)/shard_map/short_mid/pallas_call | solution.py:439
  318.6 9.1 %long_pass.3 = bf16[4,8,4,2,16,512]{5,4,3,2,1,0:T(8,128)(2,1)} custom-call(bf16[8,4,2,64,512]{4,3,2,1,0:T(8,128)(2,1)} %get-tuple-element.6.wave_ref, bf16[512,512]{1,0:T(8,128)(2,1)} %constant.45.clone.refs_2_.table_ref.refs_3_, f32[512,128]{1,0:T(8,128)} %broadcast_in_dim.56.cos_ref, f32[512,128]{1,0:T(8,128)} %broadcast_in_dim.57.sin_ref), custom_call_target="tpu_custom_call" | custom-call | tf_op jit(solution)/shard_map/long_pass/pallas_call | solution.py:486
  327.7 98.7 %exchange_2.3 = bf16[32,4,2,16,512]{4,3,2,1,0:T(8,128)(2,1)} custom-call(bf16[32,4,2,16,512]{4,3,2,1,0:T(8,128)(2,1)} %bitcast.23), custom_call_target="tpu_custom_call" | custom-call | tf_op jit(solution)/shard_map/exchange_2/pallas_call | solution.py:623
  426.4 97.6 %angle_pass.3 = bf16[4,16,2,32,512]{4,3,2,1,0:T(8,128)(2,1)} custom-call(bf16[128,2,16,512]{3,2,1,0:T(8,128)(2,1)} %bitcast.21, bf16[128,128]{1,0:T(8,128)(2,1)} %constant.46.clone.table_ref, bf16[128,128]{1,0:T(8,128)(2,1)} %constant.47.clone.table_t_ref, f32[16,128]{1,0:T(8,128)} %broadcast_in_dim.58.inv_long_ref, ...), custom_call_target="tpu_custom_call" | custom-call | tf_op jit(solution)/shard_map/angle_pass/pallas_call | solution.py:557
  523.9 0.0 copy-start
  523.9 0.0 copy-start.1
  524.0 9.5 %short_last.1 = (f32[2,64,32,512]{3,2,1,0:T(8,128)}, bf16[64,32,256]{2,1,0:T(8,128)(2,1)}) custom-call(bf16[64,2,32,512]{3,2,1,0:T(8,128)(2,1)} %bitcast.20, f32[64,32,512]{2,1,0:T(8,128)} %refs_1_.5, f32[64,32,128]{2,1,0:T(8,128)} %multiply_exponential_fusion.refs_2_), custom_call_target="tpu_custom_call" | custom-call | tf_op jit(solution)/shard_map/short_last/pallas_call | solution.py:439
  533.6 2.3 fusion
  535.9 1.0 fusion.2
  536.9 12.2 %all_to_all.5 = f32[8,64,256]{2,1,0:T(8,128)S(1)} all-to-all(f32[8,64,256]{2,1,0:T(8,128)S(1)} %bitcast.25), channel_id=1, replica_groups=mesh['grp'=4,'pen'=8] {'pen'}, dimensions={0} | all-to-all | bytes 1048576 | tf_op jit(solution)/shard_map/all_to_all | solution.py:689
  549.2 0.7 reduce_sum.19
  (20 shorter events, 0.1 us)
Async XLA Ops:
  1.3 53.7 %copy-start.5 = (f32[512]{0:T(512)S(1)}, f32[512]{0:T(512)}, u32[]{:S(2)}) copy-start(f32[512]{0:T(512)} %constant.49.clone) | copy-start | bytes 6148
  1.3 54.6 %copy-start.4 = (f32[512]{0:T(512)S(1)}, f32[512]{0:T(512)}, u32[]{:S(2)}) copy-start(f32[512]{0:T(512)} %constant.50.clone) | copy-start | bytes 6148
  65.8 98.9 %copy-start.2 = (s32[64,32]{0,1:T(8,128)S(1)}, s32[64,32]{0,1:T(8,128)}, u32[]{:S(2)}) copy-start(s32[64,32]{0,1:T(8,128)} %param.16) | copy-start | bytes 24580
  65.8 98.9 %copy-start.6 = (f32[4]{0:T(128)S(1)}, f32[4]{0:T(128)}, u32[]{:S(2)}) copy-start(f32[4]{0:T(128)} %param.17) | copy-start | bytes 52
  523.9 9.6 %copy-start = (s32[1,1,2048,2]{2,3,1,0:T(2,128)S(1)}, s32[1,1,2048,2]{2,3,1,0:T(2,128)}, u32[]{:S(2)}) copy-start(s32[1,1,2048,2]{2,3,1,0:T(2,128)} %param.19) | copy-start | bytes 49156
  523.9 9.6 %copy-start.1 = (s32[1,1,2048,2]{2,3,1,0:T(2,128)S(1)}, s32[1,1,2048,2]{2,3,1,0:T(2,128)}, u32[]{:S(2)}) copy-start(s32[1,1,2048,2]{2,3,1,0:T(2,128)} %param.18) | copy-start | bytes 49156
  523.9 9.6 %copy-start.3 = (f32[1,1,2048,2]{2,3,1,0:T(2,128)S(1)}, f32[1,1,2048,2]{2,3,1,0:T(2,128)}, u32[]{:S(2)}) copy-start(f32[1,1,2048,2]{2,3,1,0:T(2,128)} %param.20) | copy-start | bytes 49156
  533.6 2.3 copy-start.7
